TPU v7x, 256 devices: a whole 4x4x8 slice. The times are simulated.
256 devices in a mesh: mp: 2 (over y_lo), token: 4 (over x), tensor: 32 (over z, y_hi, core).
Axes of the slice: x: 4, y: 4 (y_hi: 2, y_lo: 2; y = y_hi * 2 + y_lo), z: 8, core: 2. Of those that a mesh axis runs over, the one named last changes fastest.
Arguments:
- inputs: bfloat16 [2, 1024, 4096], P('mp', 'token', 'tensor'), may hold values from -6 to 6
- cotangent: bfloat16 [2, 1024, 4096], P('mp', 'token', 'tensor'), may hold values from -6 to 6
- gate_w: bfloat16 [2, 4096, 14336], P('mp', None, 'tensor'), may hold values from -0.09375 to 0.09375
- up_w: bfloat16 [2, 4096, 14336], P('mp', None, 'tensor'), may hold values from -0.09375 to 0.09375
- down_w: bfloat16 [2, 14336, 4096], P('mp', 'tensor'), may hold values from -0.046875 to 0.046875
Outputs:
- input_grad: bfloat16 [2, 1024, 4096], P('mp', 'token', 'tensor')
- merged_gate: bfloat16 [4096, 14336], P(('mp', 'token'), 'tensor')
- merged_up: bfloat16 [4096, 14336], P(('mp', 'token'), 'tensor')
- merged_down: bfloat16 [14336, 4096], P('tensor', ('mp', 'token'))
All inputs are finite; a program needn't handle non-finite values.
Results may differ from a plain program's by a relative error of at most 0.02.
Values may be sent and summed in bfloat16 or wider, within the bound.
A program may use at most 192 MiB of HBM per device.

v0:
```python
import jax
import jax.numpy as jnp
from jax import lax
from jax.sharding import PartitionSpec as P


def square_round(value):
    wide = value.astype(jnp.float32)
    return (wide * wide).astype(jnp.bfloat16)


def contract_last(left, right):
    return lax.dot_general(
        left, right, (((1,), (1,)), ((), ())), preferred_element_type=jnp.float32
    )


def local(inputs, cotangent, gate_w, up_w, down_w):
    wgate = gate_w[0]
    wup = up_w[0]
    wdown = down_w[0]
    width = wgate.shape[0]
    hidden_cols = wgate.shape[1]
    tok_rows = inputs.shape[1]
    n_models = lax.axis_size("mp")
    n_token = lax.axis_size("token")
    eighth = width // (n_models * n_token)
    whole_feats, whole_cotan = (
        lax.all_gather(inputs, "tensor", axis=2, tiled=True),
        lax.all_gather(cotangent, "tensor", axis=2, tiled=True),
    )
    feats = whole_feats[0]
    cotan = whole_cotan[0]
    gate = jnp.dot(feats, wgate, preferred_element_type=jnp.float32)
    upval = jnp.dot(feats, wup, preferred_element_type=jnp.float32)
    dhid = contract_last(cotan, wdown)
    sig = jax.nn.sigmoid(gate)
    act = gate * sig
    hidden = (act * upval).astype(jnp.bfloat16)
    dgate = dhid * upval * sig * (1.0 + gate * (1.0 - sig))
    dup = dhid * act
    dgate_b = dgate.astype(jnp.bfloat16)
    dup_b = dup.astype(jnp.bfloat16)
    dx_terms = contract_last(dgate_b, wgate) + contract_last(dup_b, wup)
    dx_share = lax.psum_scatter(
        dx_terms.astype(jnp.bfloat16), "tensor", scatter_dimension=1, tiled=True
    )
    input_grad = dx_share[None]
    xsq = square_round(feats).reshape(tok_rows, n_models, n_token, eighth)
    gsq = square_round(cotan).reshape(tok_rows, n_models, n_token, eighth)
    dgsq = (dgate * dgate).astype(jnp.bfloat16)
    dusq = (dup * dup).astype(jnp.bfloat16)
    hsq = square_round(hidden)
    feat_rows, cotan_rows = (
        lax.all_to_all(xsq, "token", split_axis=2, concat_axis=0, tiled=True),
        lax.all_to_all(gsq, "token", split_axis=2, concat_axis=0, tiled=True),
    )
    dg_all, du_all, hid_all = (
        lax.all_gather(dgsq, "token", axis=0, tiled=True),
        lax.all_gather(dusq, "token", axis=0, tiled=True),
        lax.all_gather(hsq, "token", axis=0, tiled=True),
    )
    feat_rows = feat_rows[:, :, 0]
    cotan_rows = cotan_rows[:, :, 0]
    fisher_gate = jnp.einsum("tmd,tf->mdf", feat_rows, dg_all, preferred_element_type=jnp.float32)
    fisher_up = jnp.einsum("tmd,tf->mdf", feat_rows, du_all, preferred_element_type=jnp.float32)
    fisher_down = jnp.einsum("tmd,tf->mdf", cotan_rows, hid_all, preferred_element_type=jnp.float32)
    fisher = jnp.stack((fisher_gate, fisher_up, fisher_down), axis=0)
    position = lax.axis_index("token")
    blocks = jnp.stack((wgate, wup, wdown.T), axis=0).reshape(
        3, n_models, n_token, eighth, hidden_cols
    )
    chosen = lax.dynamic_index_in_dim(blocks, position, 2, keepdims=False)
    numer = (fisher * chosen.astype(jnp.float32)).astype(jnp.bfloat16)
    denom = fisher.astype(jnp.bfloat16)
    num_sum, den_sum = (
        lax.psum_scatter(numer, "mp", scatter_dimension=1, tiled=True).astype(jnp.float32),
        lax.psum_scatter(denom, "mp", scatter_dimension=1, tiled=True).astype(jnp.float32),
    )
    merged = (num_sum / den_sum)[:, 0].astype(jnp.bfloat16)
    return (input_grad, merged[0], merged[1], merged[2].T)


def solution(mesh):
    return jax.shard_map(
        local,
        mesh=mesh,
        in_specs=(
            P("mp", "token", "tensor"),
            P("mp", "token", "tensor"),
            P("mp", None, "tensor"),
            P("mp", None, "tensor"),
            P("mp", "tensor", None),
        ),
        out_specs=(
            P("mp", "token", "tensor"),
            P(("mp", "token"), "tensor"),
            P(("mp", "token"), "tensor"),
            P("tensor", ("mp", "token")),
        ),
        check_vma=False,
    )
```

profile of v0, /device:TPU:1, one launch (start us, length us, event | category | flops | bytes accessed | tf_op | source)
XLA Modules:
  0.0 486.1 jit_solution(1420845368890760682)
XLA Ops:
  7.2 1.6 copy.22
  8.9 1.6 copy.21
  10.5 85.1 %all-gather.5.cloned.1.call-done = bf16[1,256,4096]{1,2,0:T(8,128)(2,1)} async-done(((bf16[1,256,128]{1,2,0:T(8,128)(2,1)}), bf16[1,256,4096]{1,2,0:T(8,128)(2,1)}) %all-gather.5.cloned.1.call-update) | async-done | bytes 2097168 | tf_op jit(solution)/shard_map/all_gather | solution.py:29
  95.6 2.0 multiply_convert_fusion.1
  97.6 2.4 copy.23
  100.0 4.0 all-to-all-start
  103.9 71.6 %all-gather.3.cloned.1.call-done = bf16[1,256,4096]{1,2,0:T(8,128)(2,1)} async-done(((bf16[1,256,128]{1,2,0:T(8,128)(2,1)}), bf16[1,256,4096]{1,2,0:T(8,128)(2,1)}) %all-gather.3.cloned.1.call-update) | async-done | bytes 2097168 | tf_op jit(solution)/shard_map/all_gather | solution.py:30
  175.5 3.6 multiply_convert_fusion
  179.1 2.7 fusion.10
  181.8 4.1 copy.25
  186.0 4.0 fusion.8
  190.4 2.0 multiply_convert_fusion.5
  192.4 3.4 fusion.3
  195.8 4.5 all-to-all-start.1
  200.3 6.0 %fusion.1 = bf16[256,4096]{1,0:T(8,128)(2,1)} fusion(f32[256,4096]{1,0:T(8,128)} %fusion.3, bf16[1,4096,448]{1,2,0:T(8,128)(2,1)} %param.8, f32[256,448]{0,1:T(8,128)S(1)} %fusion.10, f32[256,448]{0,1:T(8,128)S(1)} %get-tuple-element.13), kind=kOutput, calls=%fused_computation.7 | convolution fusion | flops 942309376 | bytes 10878976 | tf_op jit(solution)/shard_map/dot_general | solution.py:13
  206.3 4.1 copy.30
  210.6 7.2 %stack.26 = bf16[1,2,4,512,448]{3,2,1,4,0:T(4,128)(2,1)} reshape(bf16[1,4096,448]{1,2,0:T(8,128)(2,1)} %param.7) | data formatting | bytes 7340032 | tf_op jit(solution)/shard_map/stack | solution.py:70
  217.8 7.2 %stack.27 = bf16[1,2,4,512,448]{3,2,1,4,0:T(4,128)(2,1)} reshape(bf16[1,4096,448]{1,2,0:T(8,128)(2,1)} %param.8) | data formatting | bytes 7340032 | tf_op jit(solution)/shard_map/stack | solution.py:70
  225.0 5.4 %copy.27 = bf16[1,2,4,512,448]{3,4,1,0,2:T(8,128)(2,1)} copy(bf16[1,2,4,512,448]{3,2,1,4,0:T(4,128)(2,1)} %stack.26) | data formatting | bytes 7340032 | tf_op jit(solution)/shard_map/stack | solution.py:70
  230.4 3.2 copy.28
  233.6 7.2 %stack.28 = bf16[1,2,4,512,448]{3,2,1,4,0:T(4,128)(2,1)} reshape(bf16[4096,448]{0,1:T(8,128)(2,1)} %bitcast.99) | data formatting | bytes 7340032 | tf_op jit(solution)/shard_map/stack | solution.py:70
  240.8 5.1 %copy.29 = bf16[1,2,4,512,448]{3,4,1,0,2:T(8,128)(2,1)} copy(bf16[1,2,4,512,448]{3,2,1,4,0:T(4,128)(2,1)} %stack.28) | data formatting | bytes 7340032 | tf_op jit(solution)/shard_map/stack | solution.py:70
  245.9 12.9 %all_gather.18 = bf16[1024,448]{0,1:T(8,128)(2,1)S(1)} all-gather(bf16[256,448]{0,1:T(8,128)(2,1)} %get-tuple-element.11), channel_id=1, replica_groups=mesh['mp'=2,'token'=4,'tensor'=32] {'token'}, dimensions={0}, use_global_device_ids=true | all-gather | bytes 1146880 | tf_op jit(solution)/shard_map/all_gather | solution.py:60
  258.8 12.3 %all_gather.17 = bf16[1024,448]{0,1:T(8,128)(2,1)} all-gather(bf16[256,448]{0,1:T(8,128)(2,1)S(1)} %get-tuple-element.6), channel_id=1, replica_groups=mesh['mp'=2,'token'=4,'tensor'=32] {'token'}, dimensions={0}, use_global_device_ids=true | all-gather | bytes 1146880 | tf_op jit(solution)/shard_map/all_gather | solution.py:59
  271.1 13.1 %all_gather.19 = bf16[1024,448]{0,1:T(8,128)(2,1)} all-gather(bf16[256,448]{0,1:T(8,128)(2,1)S(1)} %get-tuple-element.12), channel_id=1, replica_groups=mesh['mp'=2,'token'=4,'tensor'=32] {'token'}, dimensions={0}, use_global_device_ids=true | all-gather | bytes 1146880 | tf_op jit(solution)/shard_map/all_gather | solution.py:61
  285.9 1.9 copy.26
  291.6 2.1 fusion.2
  295.9 2.2 fusion
  299.3 22.0 %reduce-scatter.10.cloned.1.call-done = bf16[128,256]{1,0:T(8,128)(2,1)} async-done(((bf16[4096,256]{1,0:T(8,128)(2,1)}), bf16[128,256]{1,0:T(8,128)(2,1)}) %reduce-scatter.10.cloned.1.call-update) | async-done | bytes 65552
  321.2 1.6 copy.31
  322.8 152.8 %all-reduce.5.cloned.1.call-done = (bf16[3,2,512,448]{2,3,1,0:T(8,128)(2,1)}, bf16[3,2,512,448]{2,3,1,0:T(8,128)(2,1)}) async-done(((bf16[3,2,512,448]{2,3,1,0:T(8,128)(2,1)}, bf16[3,2,512,448]{2,3,1,0:T(8,128)(2,1)}), (bf16[3,2,512,448]{2,3,1,0:T(8,128)(2,1)}, bf16[3,2,512,448]{2,3,1,0:T(8,128)(2,1)})) %all-reduce.5.cloned.1.call-update) | async-done | bytes 5505040
  475.6 2.8 divide_convert_fusion
  (38 shorter events, 10.7 us)
Async XLA Ops:
  7.2 88.4 %all-gather.5.cloned.1.call-start = ((), (), s32[]{:S(2)}) async-start(), calls=%async_computation.4 | async-start | bytes 2162688 | tf_op jit(solution)/shard_map/all_gather | solution.py:29
  8.8 166.7 %all-gather.3.cloned.1.call-start = ((), (), s32[]{:S(2)}) async-start(), calls=%async_computation.3 | async-start | bytes 2162688 | tf_op jit(solution)/shard_map/all_gather | solution.py:30
  100.0 95.8 %all-to-all-start = ((bf16[256,2,4,512]{3,0,1,2:T(8,128)(2,1)}), bf16[256,2,4,512]{3,0,1,2:T(8,128)(2,1)S(1)}, u32[]{:S(2)}, u32[]{:S(2)}) async-start(bf16[256,2,4,512]{3,0,1,2:T(8,128)(2,1)} %copy.23), calls=%async_computation | async-start | bytes 4194304 | tf_op jit(solution)/shard_map/all_to_all | solution.py:55
  175.5 3.6 copy-start.5
  186.0 4.0 copy-start
  186.0 4.4 copy-start.6
  195.8 90.1 %all-to-all-start.1 = ((bf16[256,2,4,512]{3,0,1,2:T(8,128)(2,1)}), bf16[256,2,4,512]{3,0,1,2:T(8,128)(2,1)}, u32[]{:S(2)}, u32[]{:S(2)}) async-start(bf16[256,2,4,512]{3,0,1,2:T(8,128)(2,1)} %copy.25), calls=%async_computation.1 | async-start | bytes 4194304 | tf_op jit(solution)/shard_map/all_to_all | solution.py:56
  200.2 121.0 %reduce-scatter.10.cloned.1.call-start = ((), (), s32[]{:S(2)}) async-start(), calls=%async_computation.5 | async-start | bytes 2162688
  210.4 265.2 %all-reduce.5.cloned.1.call-start = ((), (), s32[]{:S(2)}) async-start(), calls=%async_computation.6 | async-start | bytes 11010048
  225.0 5.4 %copy-start.1 = (bf16[1,2,4,512,448]{3,2,1,4,0:T(4,128)(2,1)S(1)}, bf16[1,2,4,512,448]{3,2,1,4,0:T(4,128)(2,1)}, u32[]{:S(2)}) copy-start(bf16[1,2,4,512,448]{3,2,1,4,0:T(4,128)(2,1)} %stack.27) | copy-start | bytes 11010052
  285.8 2.2 copy-start.7
  288.1 1.2 copy-start.8
  289.2 1.2 copy-start.9
  290.4 3.3 copy-start.4
  291.5 3.3 copy-start.2
  291.6 4.3 copy-start.3
  298.0 0.7 copy-start.10
Sparse Core Ops, SparseCore 0:
  11.4 84.1 all-gather.4
  98.9 76.5 all-gather.2
  210.5 110.7 reduce-scatter.9
  324.1 151.4 all-reduce.4
where the time goes:
time: 487 us; the launch traced here: 486 us
  waiting for transfers between devices  332 us (68%)
  local copies, waits for them, and re-layouts  59.5 us (12%)
  blocking collectives  38.3 us (8%)
  matrix products  21.4 us (4%)
  between operations  13.9 us (3%)
  other arithmetic  12.7 us (3%)
  starting transfers between devices  8.77 us (2%)
    unnamed x6, waiting for transfers between devices  175 us
    all_gather x1, waiting for transfers between devices, local(): lax.all_gather(inputs, 'tensor', axis=2, tiled=True)  85.1 us
    all_gather x1, waiting for transfers between devices, local(): lax.all_gather(cotangent, 'tensor', axis=2, tiled=True)  71.6 us
    another operation x6, local copies, waits for them, and re-layouts, local(): jnp.stack((wgate, wup, wdown.T), axis=0)  35.3 us
    all_gather x1, blocking collectives, local(): lax.all_gather(hsq, 'token', axis=0, tiled=True)  13.1 us
    unnamed x27, local copies, waits for them, and re-layouts  13.1 us
    all_gather x1, blocking collectives, local(): lax.all_gather(dusq, 'token', axis=0, tiled=True)  12.9 us
    all_gather x1, blocking collectives, local(): lax.all_gather(dgsq, 'token', axis=0, tiled=True)  12.3 us
  transfers between devices with their start and end apart: 6, of which 4 were waited for; matrix products, arithmetic and copies ran while one was open for 17% of the time, Pallas kernels for 0%

commit v1 on v0

v1 whole, which is shorter than its diff:
```python
import jax
import jax.numpy as jnp
from jax import lax
from jax.experimental import pallas as pl
from jax.experimental.pallas import tpu as pltpu
from jax.sharding import PartitionSpec as P

MESH = pl.DeviceIdType.MESH
BF = jnp.bfloat16
F32 = jnp.float32
TOK = 256
HID = 448
FEAT = 128
ROWS = 512
NZ = 8
NX = 4
NT = (((1,), (1,)), ((), ()))


def kernel(
    inp, cot, gw, uw, dw,
    ig, mg, mu, md,
    xg, rg, xs, hq, gwv, uwv, dwv, wt, wr, fs, fr, nown, down, part, sib, zin, us, vin,
    acc, dgb, dub, sq, ogrd, om, omd,
    load_sem, out_sem, ring_s, ring_r, yx_s, yx_r, sf_s, sf_r, xb_s, xb_r, rf_s, rf_r,
    hq_s, hq_r, w_s, w_r, f_s, f_r, sb_s, sb_r, z_s, z_r, v_s, v_r,
):
    m = lax.axis_index("mp")
    x = lax.axis_index("token")
    k = lax.axis_index("tensor")
    z = k // 4
    yh = (k // 2) % 2
    c = k % 2
    om_ = 1 - m

    def tensor_at(zz, yy, cc):
        return {"tensor": zz * 4 + yy * 2 + cc}

    def wrap(v):
        return (v + 2 * NZ) % NZ

    def remote(src, dst, ssem, rsem, where):
        return pltpu.make_async_remote_copy(
            src_ref=src, dst_ref=dst, send_sem=ssem, recv_sem=rsem, device_id=where, device_id_type=MESH
        )

    sibling = tensor_at(z, yh, 1 - c)
    y_mate = tensor_at(z, 1 - yh, c)
    mp_mate = {"mp": om_}

    loads = [
        pltpu.make_async_copy(inp.at[0], xg.at[0, c, z, yh], load_sem.at[0]),
        pltpu.make_async_copy(cot.at[0], xg.at[1, c, z, yh], load_sem.at[1]),
        pltpu.make_async_copy(gw.at[0], gwv, load_sem.at[2]),
        pltpu.make_async_copy(uw.at[0], uwv, load_sem.at[3]),
        pltpu.make_async_copy(dw.at[0], dwv, load_sem.at[4]),
    ]
    for ld in loads:
        ld.start()

    barrier = pltpu.get_barrier_semaphore()

    def greet(where):
        pl.semaphore_signal(barrier, inc=1, device_id=where, device_id_type=MESH)

    greet(sibling)
    greet(y_mate)
    greet(mp_mate)
    for o in range(1, NX):
        greet({"token": (x + o) % NX})
    for o in range(1, NZ):
        greet(tensor_at((z + o) % NZ, yh, c))
    pl.semaphore_wait(barrier, 3 + (NX - 1) + (NZ - 1))

    def yx_copy(a):
        blk = xg.at[a, c, z, yh]
        return remote(blk, blk, yx_s.at[a], yx_r.at[a], y_mate)

    def ring_copy(a, d, s, u):
        yy = yh if u == 0 else 1 - yh
        zb = wrap(z - (s - 1)) if d == 0 else wrap(z + (s - 1))
        to = wrap(z + 1) if d == 0 else wrap(z - 1)
        blk = xg.at[a, c, zb, yy]
        return remote(blk, blk, ring_s.at[a, d, s, u], ring_r.at[a, d, s, u], tensor_at(to, yh, c))

    def sib_fwd(a, zb, slot):
        blk = xg.at[a, c, zb]
        return remote(blk, blk, sf_s.at[a, slot], sf_r.at[a, slot], sibling)

    def xb_copy(a, zb, slot):
        t = zb % NX
        o = (x - t + NX) % NX - 1
        return remote(
            xg.at[a, c, zb], rg.at[a, c, x, zb // NX], xb_s.at[a, slot], xb_r.at[a, o, zb // NX], {"token": t}
        )

    def xb_start(a, zb, slot):
        @pl.when(zb % NX != x)
        def _():
            xb_copy(a, zb, slot).start()

    def consume(a, zb):
        blk = jnp.concatenate([xg[a, 0, zb, 0], xg[a, 1, zb, 0], xg[a, 0, zb, 1], xg[a, 1, zb, 1]], axis=1)
        at = pl.multiple_of(zb * ROWS, ROWS)
        if a == 0:
            acc[0] += jnp.dot(blk, gwv[pl.ds(at, ROWS), :], preferred_element_type=F32)
            acc[1] += jnp.dot(blk, uwv[pl.ds(at, ROWS), :], preferred_element_type=F32)
        else:
            acc[2] += lax.dot_general(blk, dwv[:, pl.ds(at, ROWS)], NT, preferred_element_type=F32)

    def w_copy(i):
        if i == 2:
            src = dwv.at[:, pl.ds(pl.multiple_of((om_ * NX + x) * ROWS, ROWS), ROWS)]
        else:
            src = wt.at[i, om_]
        return remote(src, wr.at[i], w_s.at[i], w_r.at[i], mp_mate)

    def turn_weights(i, half):
        w = gwv if i == 0 else uwv
        at = pl.multiple_of((half * NX + x) * ROWS, ROWS)
        wt[i, half] = w[pl.ds(at, ROWS), :].T

    for a in range(2):
        loads[a].wait()
    for a in range(2):
        yx_copy(a).start()
        for d in range(2):
            ring_copy(a, d, 1, 0).start()
    acc[...] = jnp.zeros_like(acc)
    loads[4].wait()
    w_copy(2).start()
    for a in range(2):
        yx_copy(a).wait_recv()
        for d in range(2):
            ring_copy(a, d, 1, 1).start()
        sib_fwd(a, z, 0).start()
        xb_start(a, z, 0)
    loads[2].wait()
    loads[3].wait()
    turn_weights(0, om_)
    w_copy(0).start()
    for a in range(2):
        sib_fwd(a, z, 0).wait_recv()
        consume(a, z)

    def ring_step(s, _):
        lo, hi = wrap(z - s), wrap(z + s)
        for a in range(2):
            for u in range(2):
                for d in range(2):
                    ring_copy(a, d, s, u).wait_recv()

                    @pl.when(jnp.logical_or(s < 3, a == d))
                    def _():
                        ring_copy(a, d, s + 1, u).start()
            sib_fwd(a, lo, 2 * s - 1).start()
            sib_fwd(a, hi, 2 * s).start()
            xb_start(a, lo, 2 * s - 1)
            xb_start(a, hi, 2 * s)

        @pl.when(s == 1)
        def _():
            turn_weights(1, om_)
            w_copy(1).start()

        for a in range(2):
            sib_fwd(a, lo, 2 * s - 1).wait_recv()
            consume(a, lo)
            sib_fwd(a, hi, 2 * s).wait_recv()
            consume(a, hi)
        return 0

    lax.fori_loop(1, 4, ring_step, 0)
    far = wrap(z + 4)
    for a in range(2):
        for u in range(2):
            ring_copy(a, a, 4, u).wait_recv()
        sib_fwd(a, far, 7).start()
        xb_start(a, far, 7)
    for a in range(2):
        sib_fwd(a, far, 7).wait_recv()
        consume(a, far)

    def hidden_rows(j, _):
        rows = pl.ds(pl.multiple_of(j * 32, 32), 32)
        gate, up, dh = acc[0, rows, :], acc[1, rows, :], acc[2, rows, :]
        sig = 1.0 / (1.0 + jnp.exp(-gate))
        act = gate * sig
        hid = (act * up).astype(BF).astype(F32)
        dg = dh * up * sig * (1.0 + gate * (1.0 - sig))
        du = dh * act
        dgb[rows, :] = dg.astype(BF)
        dub[rows, :] = du.astype(BF)
        sq[0, rows, :] = dg * dg
        sq[1, rows, :] = du * du
        sq[2, rows, :] = hid * hid
        return 0

    lax.fori_loop(0, TOK // 32, hidden_rows, 0)

    def hq_copy(i, o):
        blk = hq.at[i, x]
        return remote(blk, blk, hq_s.at[i, o - 1], hq_r.at[i, o - 1], {"token": (x + o) % NX})

    for i in range(3):
        hq[i, x] = sq[i].T.astype(BF)
        for o in range(1, NX):
            hq_copy(i, o).start()

    def rg_copy(a, o, half):
        blk = rg.at[a, c, (x + o) % NX, half]
        return remote(blk, blk, rf_s.at[a, o - 1, half], rf_r.at[a, o - 1, half], sibling)

    def rg_landed(a, o, half):
        blk = rg.at[a, c, (x + o) % NX, half]
        return remote(blk, blk, xb_s.at[a, 0], xb_r.at[a, o - 1, half], sibling)

    for a in range(2):
        for o in range(1, NX):
            for half in range(2):
                rg_landed(a, o, half).wait_recv()
                rg_copy(a, o, half).start()

    def grad_block(zb, _):
        at = pl.multiple_of(zb * ROWS, ROWS)
        val = lax.dot_general(dgb[...], gwv[pl.ds(at, ROWS), :], NT, preferred_element_type=F32)
        val += lax.dot_general(dub[...], uwv[pl.ds(at, ROWS), :], NT, preferred_element_type=F32)
        val = val.astype(BF)
        for yy in range(2):
            for cc in range(2):
                part[cc, zb, yy] = val[:, (yy * 2 + cc) * FEAT : (yy * 2 + cc + 1) * FEAT]
        return 0

    lax.fori_loop(0, NZ, grad_block, 0)
    sib_part = remote(part.at[1 - c], sib, sb_s.at[0], sb_r.at[0], sibling)
    sib_part.start()

    def square(v):
        v = v.astype(F32)
        return (v * v).astype(BF)

    for a in range(2):
        for o in range(NX):
            src = (x + o) % NX
            at = pl.multiple_of(src * TOK, TOK)
            for half in range(2):
                if o:
                    rg_copy(a, o, half).wait_recv()
                for yy in range(2):
                    for cc in range(2):
                        v = xg[a, cc, half * NX + x, yy] if o == 0 else rg[a, cc, src, half, yy]
                        lane = (yy * 2 + cc) * FEAT
                        xs[a, half, pl.ds(at, TOK), lane : lane + FEAT] = square(v)

    sib_part.wait_recv()

    def z_copy(o):
        to = (z + o) % NZ
        return remote(sib.at[to], zin.at[z], z_s.at[o - 1], z_r.at[o - 1], tensor_at(to, yh, c))

    def z_landed(o):
        blk = zin.at[wrap(z - o)]
        return remote(blk, blk, z_s.at[o - 1], z_r.at[o - 1], tensor_at(wrap(z - o), yh, c))

    for o in range(1, NZ + 1):
        to = (z + o) % NZ
        sib[to] = (sib[to].astype(F32) + part[c, to].astype(F32)).astype(BF)
        if o < NZ:
            z_copy(o).start()

    for i in range(2):
        turn_weights(i, m)

    def f_copy(i):
        return remote(fs.at[i], fr.at[i], f_s.at[i], f_r.at[i], mp_mate)

    def own_weights(i):
        if i == 2:
            return dwv[:, pl.ds(pl.multiple_of((m * NX + x) * ROWS, ROWS), ROWS)]
        return wt[i, m]

    for i in range(3):
        for o in range(1, NX):
            blk = hq.at[i, (x - o + NX) % NX]
            remote(blk, blk, hq_s.at[i, o - 1], hq_r.at[i, o - 1], {"token": (x - o + NX) % NX}).wait_recv()
        a = 1 if i == 2 else 0
        lhs = jnp.concatenate([hq[i, t] for t in range(NX)], axis=1)
        fs[i] = jnp.dot(lhs, xs[a, om_], preferred_element_type=F32).astype(BF)
        f_copy(i).start()
        fo = jnp.dot(lhs, xs[a, m], preferred_element_type=F32)
        nown[i] = (fo * own_weights(i).astype(F32)).astype(BF)
        down[i] = fo.astype(BF)

    total = sib[z].astype(F32)
    for o in range(1, NZ):
        z_landed(o).wait_recv()
        total += zin[wrap(z - o)].astype(F32)
    us[...] = total.astype(BF)
    v_copy = remote(us.at[1 - yh], vin, v_s.at[0], v_r.at[0], y_mate)
    v_copy.start()

    outs = []
    for i in range(3):
        remote(fr.at[i], fr.at[i], f_s.at[i], f_r.at[i], mp_mate).wait_recv()
        remote(wr.at[i], wr.at[i], w_s.at[i], w_r.at[i], mp_mate).wait_recv()
        if i == 2:
            v_copy.wait_recv()
            ogrd[...] = (us[yh].astype(F32) + vin[...].astype(F32)).astype(BF)
            outs.append(pltpu.make_async_copy(ogrd, ig.at[0], out_sem.at[3]))
            outs[-1].start()
        other = fr[i].astype(F32)
        num = nown[i].astype(F32) + (other * wr[i].astype(F32)).astype(BF).astype(F32)
        merged = num / (down[i].astype(F32) + other)
        if i == 2:
            omd[...] = merged.astype(BF)
        else:
            om[i] = merged.astype(BF).T
        outs.append(pltpu.make_async_copy(om.at[i] if i < 2 else omd, (mg, mu, md)[i], out_sem.at[i]))
        outs[-1].start()

    for a in range(2):
        yx_copy(a).wait_send()
        for u in range(2):
            for d in range(2):
                for s in range(1, 5):
                    if s < 4 or a == d:
                        ring_copy(a, d, s, u).wait_send()
        for slot in range(8):
            sib_fwd(a, z, slot).wait_send()
            zb = wrap(z + (0, -1, 1, -2, 2, -3, 3, 4)[slot])

            @pl.when(zb % NX != x)
            def _():
                xb_copy(a, zb, slot).wait_send()

        for o in range(1, NX):
            for half in range(2):
                rg_copy(a, o, half).wait_send()
    for i in range(3):
        w_copy(i).wait_send()
        f_copy(i).wait_send()
        for o in range(1, NX):
            hq_copy(i, o).wait_send()
    sib_part.wait_send()
    for o in range(1, NZ):
        z_copy(o).wait_send()
    v_copy.wait_send()
    for o in outs:
        o.wait()


def local(*args):
    dma = pltpu.SemaphoreType.DMA
    vm = pltpu.VMEM
    return pl.pallas_call(
        kernel,
        out_shape=(
            jax.ShapeDtypeStruct((1, TOK, FEAT), BF),
            jax.ShapeDtypeStruct((ROWS, HID), BF),
            jax.ShapeDtypeStruct((ROWS, HID), BF),
            jax.ShapeDtypeStruct((HID, ROWS), BF),
        ),
        in_specs=[pl.BlockSpec(memory_space=pl.ANY)] * 5,
        out_specs=[pl.BlockSpec(memory_space=pl.ANY)] * 4,
        scratch_shapes=[
            vm((2, 2, NZ, 2, TOK, FEAT), BF),
            vm((2, 2, NX, 2, 2, TOK, FEAT), BF),
            vm((2, 2, NX * TOK, ROWS), BF),
            vm((3, NX, HID, TOK), BF),
            vm((NZ * ROWS, HID), BF),
            vm((NZ * ROWS, HID), BF),
            vm((HID, NZ * ROWS), BF),
            vm((2, 2, HID, ROWS), BF),
            vm((3, HID, ROWS), BF),
            vm((3, HID, ROWS), BF),
            vm((3, HID, ROWS), BF),
            vm((3, HID, ROWS), BF),
            vm((3, HID, ROWS), BF),
            vm((2, NZ, 2, TOK, FEAT), BF),
            vm((NZ, 2, TOK, FEAT), BF),
            vm((NZ, 2, TOK, FEAT), BF),
            vm((2, TOK, FEAT), BF),
            vm((TOK, FEAT), BF),
            vm((3, TOK, HID), F32),
            vm((TOK, HID), BF),
            vm((TOK, HID), BF),
            vm((3, TOK, HID), F32),
            vm((TOK, FEAT), BF),
            vm((2, ROWS, HID), BF),
            vm((HID, ROWS), BF),
            dma((5,)), dma((4,)),
            dma((2, 2, 5, 2)), dma((2, 2, 5, 2)),
            dma((2,)), dma((2,)),
            dma((2, 8)), dma((2, 8)),
            dma((2, 8)), dma((2, 3, 2)),
            dma((2, 3, 2)), dma((2, 3, 2)),
            dma((3, 3)), dma((3, 3)),
            dma((3,)), dma((3,)),
            dma((3,)), dma((3,)),
            dma((1,)), dma((1,)),
            dma((7,)), dma((7,)),
            dma((1,)), dma((1,)),
        ],
        compiler_params=pltpu.CompilerParams(collective_id=0, has_side_effects=True, vmem_limit_bytes=58 << 20),
        cost_estimate=pl.CostEstimate(flops=7_500_000_000, bytes_accessed=16_000_000, transcendentals=120_000),
        name="fisher_merge",
    )(*args)


def solution(mesh):
    return jax.shard_map(
        local,
        mesh=mesh,
        in_specs=(
            P("mp", "token", "tensor"),
            P("mp", "token", "tensor"),
            P("mp", None, "tensor"),
            P("mp", None, "tensor"),
            P("mp", "tensor", None),
        ),
        out_specs=(
            P("mp", "token", "tensor"),
            P(("mp", "token"), "tensor"),
            P(("mp", "token"), "tensor"),
            P("tensor", ("mp", "token")),
        ),
        check_vma=False,
    )
```

time: 487 us -> 120 us (0.25)
  the two profiles are of different devices: /device:TPU:1 before, /device:TPU:42 now
where the time goes in v1:
time: 120 us; the launch traced here: 119 us
  Pallas kernels  98.4 us (82%)
  local copies, waits for them, and re-layouts  20.2 us (17%)
    pallas_call x1, Pallas kernels, local(): pl.pallas_call(kernel, out_shape=(jax.ShapeDtypeStruct((1, TOK, FEAT), BF...  98.4 us
    unnamed x4, local copies, waits for them, and re-layouts  16.2 us
    pallas_call x2, local copies, waits for them, and re-layouts, local(): pl.pallas_call(kernel, out_shape=(jax.ShapeDtypeStruct((1, TOK, FEAT), BF...  4.01 us

profile of v1, /device:TPU:42, one launch (start us, length us, event | category | flops | bytes accessed | tf_op | source)
XLA Modules:
  0.0 119.2 jit_solution(1467000227862400134)
XLA Ops:
  0.6 6.4 %copy.9.gw = bf16[1,4096,448]{2,1,0:T(8,128)(2,1)} copy(bf16[1,4096,448]{1,2,0:T(8,128)(2,1)} %param.7) | data formatting | bytes 7340032 | tf_op args[2]
  7.0 6.5 %copy.10.uw = bf16[1,4096,448]{2,1,0:T(8,128)(2,1)} copy(bf16[1,4096,448]{1,2,0:T(8,128)(2,1)} %param.8) | data formatting | bytes 7340032 | tf_op args[3]
  13.5 98.4 %fisher_merge.1 = (bf16[1,256,128]{2,1,0:T(8,128)(2,1)}, bf16[512,448]{1,0:T(8,128)(2,1)}, bf16[512,448]{1,0:T(8,128)(2,1)}, bf16[448,512]{1,0:T(8,128)(2,1)}) custom-call(bf16[1,256,128]{2,1,0:T(8,128)(2,1)} %inp.1, bf16[1,256,128]{2,1,0:T(8,128)(2,1)} %cot.1, bf16[1,4096,448]{2,1,0:T(8,128)(2,1)} %copy.9.gw, bf16[1,4096,448]{2,1,0:T(8,128)(2,1)} %copy.10.uw, ...), custom_call_target="tpu_custom_call" | custom-call | flops 7500000256 | bytes 16000000 | tf_op jit(solution)/shard_map/fisher_merge/pallas_call | solution.py:355
  111.9 2.0 %copy.11 = bf16[512,448]{0,1:T(8,128)(2,1)} copy(bf16[512,448]{1,0:T(8,128)(2,1)} %get-tuple-element.5) | data formatting | bytes 917504 | tf_op jit(solution)/shard_map/fisher_merge/pallas_call | solution.py:355
  113.9 2.0 %copy.12 = bf16[512,448]{0,1:T(8,128)(2,1)} copy(bf16[512,448]{1,0:T(8,128)(2,1)} %get-tuple-element.6) | data formatting | bytes 917504 | tf_op jit(solution)/shard_map/fisher_merge/pallas_call | solution.py:355
  115.9 1.5 %copy.15 = bf16[1,256,128]{2,1,0:T(8,128)(2,1)} copy(bf16[1,256,128]{2,1,0:T(8,128)(2,1)} %get-tuple-element.12) | data formatting | bytes 131072
  117.4 1.8 %copy.16 = bf16[448,512]{1,0:T(8,128)(2,1)} copy(bf16[448,512]{1,0:T(8,128)(2,1)} %get-tuple-element.15) | data formatting | bytes 917504

commit v2 on v1

--- a/solution.py
+++ b/solution.py
@@ -19,9 +19,9 @@
 
 def kernel(
     inp, cot, gw, uw, dw,
-    ig, mg, mu, md,
-    xg, rg, xs, hq, gwv, uwv, dwv, wt, wr, fs, fr, nown, down, part, sib, zin, us, vin,
-    acc, dgb, dub, sq, ogrd, om, omd,
+    ig, mt,
+    xg, rg, xs, hq, wv, wr, fs, fr, nown, down, part, sib, zin, us, vin,
+    acc, dgt, dut, dgb, dub, ogrd, om,
     load_sem, out_sem, ring_s, ring_r, yx_s, yx_r, sf_s, sf_r, xb_s, xb_r, rf_s, rf_r,
     hq_s, hq_r, w_s, w_r, f_s, f_r, sb_s, sb_r, z_s, z_r, v_s, v_r,
 ):
@@ -51,9 +51,9 @@
     loads = [
         pltpu.make_async_copy(inp.at[0], xg.at[0, c, z, yh], load_sem.at[0]),
         pltpu.make_async_copy(cot.at[0], xg.at[1, c, z, yh], load_sem.at[1]),
-        pltpu.make_async_copy(gw.at[0], gwv, load_sem.at[2]),
-        pltpu.make_async_copy(uw.at[0], uwv, load_sem.at[3]),
-        pltpu.make_async_copy(dw.at[0], dwv, load_sem.at[4]),
+        pltpu.make_async_copy(gw.at[0], wv.at[0], load_sem.at[2]),
+        pltpu.make_async_copy(uw.at[0], wv.at[1], load_sem.at[3]),
+        pltpu.make_async_copy(dw.at[0], wv.at[2], load_sem.at[4]),
     ]
     for ld in loads:
         ld.start()
@@ -102,23 +102,14 @@
     def consume(a, zb):
         blk = jnp.concatenate([xg[a, 0, zb, 0], xg[a, 1, zb, 0], xg[a, 0, zb, 1], xg[a, 1, zb, 1]], axis=1)
         at = pl.multiple_of(zb * ROWS, ROWS)
-        if a == 0:
-            acc[0] += jnp.dot(blk, gwv[pl.ds(at, ROWS), :], preferred_element_type=F32)
-            acc[1] += jnp.dot(blk, uwv[pl.ds(at, ROWS), :], preferred_element_type=F32)
-        else:
-            acc[2] += lax.dot_general(blk, dwv[:, pl.ds(at, ROWS)], NT, preferred_element_type=F32)
+        for i in (0, 1) if a == 0 else (2,):
+            acc[i] += lax.dot_general(wv[i, :, pl.ds(at, ROWS)], blk, NT, preferred_element_type=F32)
+
+    def merge_rows(half):
+        return pl.ds(pl.multiple_of((half * NX + x) * ROWS, ROWS), ROWS)
 
     def w_copy(i):
-        if i == 2:
-            src = dwv.at[:, pl.ds(pl.multiple_of((om_ * NX + x) * ROWS, ROWS), ROWS)]
-        else:
-            src = wt.at[i, om_]
-        return remote(src, wr.at[i], w_s.at[i], w_r.at[i], mp_mate)
-
-    def turn_weights(i, half):
-        w = gwv if i == 0 else uwv
-        at = pl.multiple_of((half * NX + x) * ROWS, ROWS)
-        wt[i, half] = w[pl.ds(at, ROWS), :].T
+        return remote(wv.at[i, :, merge_rows(om_)], wr.at[i], w_s.at[i], w_r.at[i], mp_mate)
 
     for a in range(2):
         loads[a].wait()
@@ -127,18 +118,17 @@
         for d in range(2):
             ring_copy(a, d, 1, 0).start()
     acc[...] = jnp.zeros_like(acc)
-    loads[4].wait()
-    w_copy(2).start()
+    loads[2].wait()
+    w_copy(0).start()
     for a in range(2):
         yx_copy(a).wait_recv()
         for d in range(2):
             ring_copy(a, d, 1, 1).start()
         sib_fwd(a, z, 0).start()
         xb_start(a, z, 0)
-    loads[2].wait()
-    loads[3].wait()
-    turn_weights(0, om_)
-    w_copy(0).start()
+    for i in (1, 2):
+        loads[2 + i].wait()
+        w_copy(i).start()
     for a in range(2):
         sib_fwd(a, z, 0).wait_recv()
         consume(a, z)
@@ -158,11 +148,6 @@
             xb_start(a, lo, 2 * s - 1)
             xb_start(a, hi, 2 * s)
 
-        @pl.when(s == 1)
-        def _():
-            turn_weights(1, om_)
-            w_copy(1).start()
-
         for a in range(2):
             sib_fwd(a, lo, 2 * s - 1).wait_recv()
             consume(a, lo)
@@ -182,28 +167,27 @@
         consume(a, far)
 
     def hidden_rows(j, _):
-        rows = pl.ds(pl.multiple_of(j * 32, 32), 32)
+        rows = pl.ds(pl.multiple_of(j * 64, 64), 64)
         gate, up, dh = acc[0, rows, :], acc[1, rows, :], acc[2, rows, :]
         sig = 1.0 / (1.0 + jnp.exp(-gate))
         act = gate * sig
         hid = (act * up).astype(BF).astype(F32)
         dg = dh * up * sig * (1.0 + gate * (1.0 - sig))
         du = dh * act
-        dgb[rows, :] = dg.astype(BF)
-        dub[rows, :] = du.astype(BF)
-        sq[0, rows, :] = dg * dg
-        sq[1, rows, :] = du * du
-        sq[2, rows, :] = hid * hid
+        dgt[rows, :] = dg.astype(BF)
+        dut[rows, :] = du.astype(BF)
+        hq[0, x, rows, :] = (dg * dg).astype(BF)
+        hq[1, x, rows, :] = (du * du).astype(BF)
+        hq[2, x, rows, :] = (hid * hid).astype(BF)
         return 0
 
-    lax.fori_loop(0, TOK // 32, hidden_rows, 0)
+    lax.fori_loop(0, HID // 64, hidden_rows, 0)
 
     def hq_copy(i, o):
         blk = hq.at[i, x]
         return remote(blk, blk, hq_s.at[i, o - 1], hq_r.at[i, o - 1], {"token": (x + o) % NX})
 
     for i in range(3):
-        hq[i, x] = sq[i].T.astype(BF)
         for o in range(1, NX):
             hq_copy(i, o).start()
 
@@ -221,10 +205,13 @@
                 rg_landed(a, o, half).wait_recv()
                 rg_copy(a, o, half).start()
 
+    dgb[...] = dgt[...].T
+    dub[...] = dut[...].T
+
     def grad_block(zb, _):
         at = pl.multiple_of(zb * ROWS, ROWS)
-        val = lax.dot_general(dgb[...], gwv[pl.ds(at, ROWS), :], NT, preferred_element_type=F32)
-        val += lax.dot_general(dub[...], uwv[pl.ds(at, ROWS), :], NT, preferred_element_type=F32)
+        val = jnp.dot(dgb[...], wv[0, :, pl.ds(at, ROWS)], preferred_element_type=F32)
+        val += jnp.dot(dub[...], wv[1, :, pl.ds(at, ROWS)], preferred_element_type=F32)
         val = val.astype(BF)
         for yy in range(2):
             for cc in range(2):
@@ -268,16 +255,8 @@
         if o < NZ:
             z_copy(o).start()
 
-    for i in range(2):
-        turn_weights(i, m)
-
     def f_copy(i):
         return remote(fs.at[i], fr.at[i], f_s.at[i], f_r.at[i], mp_mate)
-
-    def own_weights(i):
-        if i == 2:
-            return dwv[:, pl.ds(pl.multiple_of((m * NX + x) * ROWS, ROWS), ROWS)]
-        return wt[i, m]
 
     for i in range(3):
         for o in range(1, NX):
@@ -288,7 +267,7 @@
         fs[i] = jnp.dot(lhs, xs[a, om_], preferred_element_type=F32).astype(BF)
         f_copy(i).start()
         fo = jnp.dot(lhs, xs[a, m], preferred_element_type=F32)
-        nown[i] = (fo * own_weights(i).astype(F32)).astype(BF)
+        nown[i] = (fo * wv[i, :, merge_rows(m)].astype(F32)).astype(BF)
         down[i] = fo.astype(BF)
 
     total = sib[z].astype(F32)
@@ -311,11 +290,8 @@
         other = fr[i].astype(F32)
         num = nown[i].astype(F32) + (other * wr[i].astype(F32)).astype(BF).astype(F32)
         merged = num / (down[i].astype(F32) + other)
-        if i == 2:
-            omd[...] = merged.astype(BF)
-        else:
-            om[i] = merged.astype(BF).T
-        outs.append(pltpu.make_async_copy(om.at[i] if i < 2 else omd, (mg, mu, md)[i], out_sem.at[i]))
+        om[i] = merged.astype(BF)
+        outs.append(pltpu.make_async_copy(om.at[i], mt.at[i], out_sem.at[i]))
         outs[-1].start()
 
     for a in range(2):
@@ -349,28 +325,32 @@
         o.wait()
 
 
-def local(*args):
+def hand_out(ig, mt, ig_out, mg, mu, md, sem):
+    copies = [pltpu.make_async_copy(ig, ig_out, sem.at[3])]
+    copies += [pltpu.make_async_copy(mt.at[i], (mg, mu, md)[i], sem.at[i]) for i in range(3)]
+    for cp in copies:
+        cp.start()
+    for cp in copies:
+        cp.wait()
+
+
+def local(inputs, cotangent, gate_w, up_w, down_w):
     dma = pltpu.SemaphoreType.DMA
     vm = pltpu.VMEM
-    return pl.pallas_call(
+    ig, mt = pl.pallas_call(
         kernel,
         out_shape=(
             jax.ShapeDtypeStruct((1, TOK, FEAT), BF),
-            jax.ShapeDtypeStruct((ROWS, HID), BF),
-            jax.ShapeDtypeStruct((ROWS, HID), BF),
-            jax.ShapeDtypeStruct((HID, ROWS), BF),
+            jax.ShapeDtypeStruct((3, HID, ROWS), BF),
         ),
         in_specs=[pl.BlockSpec(memory_space=pl.ANY)] * 5,
-        out_specs=[pl.BlockSpec(memory_space=pl.ANY)] * 4,
+        out_specs=[pl.BlockSpec(memory_space=pl.ANY)] * 2,
         scratch_shapes=[
             vm((2, 2, NZ, 2, TOK, FEAT), BF),
             vm((2, 2, NX, 2, 2, TOK, FEAT), BF),
             vm((2, 2, NX * TOK, ROWS), BF),
             vm((3, NX, HID, TOK), BF),
-            vm((NZ * ROWS, HID), BF),
-            vm((NZ * ROWS, HID), BF),
-            vm((HID, NZ * ROWS), BF),
-            vm((2, 2, HID, ROWS), BF),
+            vm((3, HID, NZ * ROWS), BF),
             vm((3, HID, ROWS), BF),
             vm((3, HID, ROWS), BF),
             vm((3, HID, ROWS), BF),
@@ -381,13 +361,13 @@
             vm((NZ, 2, TOK, FEAT), BF),
             vm((2, TOK, FEAT), BF),
             vm((TOK, FEAT), BF),
-            vm((3, TOK, HID), F32),
+            vm((3, HID, TOK), F32),
+            vm((HID, TOK), BF),
+            vm((HID, TOK), BF),
             vm((TOK, HID), BF),
             vm((TOK, HID), BF),
-            vm((3, TOK, HID), F32),
             vm((TOK, FEAT), BF),
-            vm((2, ROWS, HID), BF),
-            vm((HID, ROWS), BF),
+            vm((3, HID, ROWS), BF),
             dma((5,)), dma((4,)),
             dma((2, 2, 5, 2)), dma((2, 2, 5, 2)),
             dma((2,)), dma((2,)),
@@ -404,7 +384,16 @@
         compiler_params=pltpu.CompilerParams(collective_id=0, has_side_effects=True, vmem_limit_bytes=58 << 20),
         cost_estimate=pl.CostEstimate(flops=7_500_000_000, bytes_accessed=16_000_000, transcendentals=120_000),
         name="fisher_merge",
-    )(*args)
+    )(inputs, cotangent, gate_w.swapaxes(1, 2), up_w.swapaxes(1, 2), down_w)
+    ig, mg, mu, md = pl.pallas_call(
+        hand_out,
+        out_shape=(jax.ShapeDtypeStruct((1, TOK, FEAT), BF),) + (jax.ShapeDtypeStruct((HID, ROWS), BF),) * 3,
+        in_specs=[pl.BlockSpec(memory_space=pltpu.VMEM)] * 2,
+        out_specs=[pl.BlockSpec(memory_space=pl.ANY)] * 4,
+        scratch_shapes=[dma((4,))],
+        name="hand_out",
+    )(ig, mt)
+    return ig, mg.T, mu.T, md
 
 
 def solution(mesh):

time: 120 us -> 101 us (0.84)
  local copies, waits for them, and re-layouts: 20.2 us -> 0 us
  Pallas kernels: 98.4 us -> 101 us
    unnamed x4 -> x0, local copies, waits for them, and re-layouts: 16.2 us -> none
    pallas_call x2 -> x0, local copies, waits for them, and re-layouts: 4.01 us -> none  [local(): pl.pallas_call(kernel, out_shape=(jax.ShapeDtypeStruct((1, TOK, FEAT), BF...]
    pallas_call x0 -> x1, Pallas kernels: none -> 2.5 us  [local(): pl.pallas_call(hand_out, out_shape=(jax.ShapeDtypeStruct((1, TOK, FEAT),...]
where the time goes in v2:
time: 101 us
  Pallas kernels  101 us (100%)
    pallas_call x1, Pallas kernels, local(): pl.pallas_call(kernel, out_shape=(jax.ShapeDtypeStruct((1, TOK, FEAT), BF...  98.1 us
    pallas_call x1, Pallas kernels, local(): pl.pallas_call(hand_out, out_shape=(jax.ShapeDtypeStruct((1, TOK, FEAT),...  2.5 us

profile of v2, /device:TPU:42, one launch (start us, length us, event | category | flops | bytes accessed | tf_op | source)
XLA Modules:
  0.0 101.2 jit_solution(7117143734563829846)
XLA Ops:
  0.6 98.1 %fisher_merge.1 = (bf16[1,256,128]{2,1,0:T(8,128)(2,1)}, bf16[3,448,512]{2,1,0:T(8,128)(2,1)}) custom-call(bf16[1,256,128]{2,1,0:T(8,128)(2,1)} %inp.1, bf16[1,256,128]{2,1,0:T(8,128)(2,1)} %cot.1, bf16[1,448,4096]{2,1,0:T(8,128)(2,1)} %bitcast.4, bf16[1,448,4096]{2,1,0:T(8,128)(2,1)} %bitcast.5, bf16[1,448,4096]{2,1,0:T(8,128)(2,1)} %dw.1), custom_call_target="tpu_custom_call" | custom-call | flops 7500000256 | bytes 16000000 | tf_op jit(solution)/shard_map/fisher_merge/pallas_call | solution.py:340
  98.7 2.5 %hand_out.1 = (bf16[1,256,128]{2,1,0:T(8,128)(2,1)}, bf16[448,512]{1,0:T(8,128)(2,1)}, bf16[448,512]{1,0:T(8,128)(2,1)}, bf16[448,512]{1,0:T(8,128)(2,1)}) custom-call(bf16[1,256,128]{2,1,0:T(8,128)(2,1)} %get-tuple-element.10.ig, bf16[3,448,512]{2,1,0:T(8,128)(2,1)} %get-tuple-element.11.mt), custom_call_target="tpu_custom_call" | custom-call | tf_op jit(solution)/shard_map/hand_out/pallas_call | solution.py:388

commit v3 on v2

--- a/solution.py
+++ b/solution.py
@@ -14,6 +14,9 @@
 ROWS = 512
 NZ = 8
 NX = 4
+HALF = HID // 2
+PIECES = 6
+LATE = 3
 NT = (((1,), (1,)), ((), ()))
 
 
@@ -21,8 +24,8 @@
     inp, cot, gw, uw, dw,
     ig, mt,
     xg, rg, xs, hq, wv, wr, fs, fr, nown, down, part, sib, zin, us, vin,
-    acc, dgt, dut, dgb, dub, ogrd, om,
-    load_sem, out_sem, ring_s, ring_r, yx_s, yx_r, sf_s, sf_r, xb_s, xb_r, rf_s, rf_r,
+    acc, dgt, dut, dgb, dub,
+    load_sem, ring_s, ring_r, yx_s, yx_r, sf_s, sf_r, xb_s, xb_r, rf_s, rf_r,
     hq_s, hq_r, w_s, w_r, f_s, f_r, sb_s, sb_r, z_s, z_r, v_s, v_r,
 ):
     m = lax.axis_index("mp")
@@ -68,9 +71,9 @@
     greet(mp_mate)
     for o in range(1, NX):
         greet({"token": (x + o) % NX})
-    for o in range(1, NZ):
+    for o in (1, NZ - 1):
         greet(tensor_at((z + o) % NZ, yh, c))
-    pl.semaphore_wait(barrier, 3 + (NX - 1) + (NZ - 1))
+    pl.semaphore_wait(barrier, 3 + (NX - 1) + 2)
 
     def yx_copy(a):
         blk = xg.at[a, c, z, yh]
@@ -145,8 +148,16 @@
                         ring_copy(a, d, s + 1, u).start()
             sib_fwd(a, lo, 2 * s - 1).start()
             sib_fwd(a, hi, 2 * s).start()
-            xb_start(a, lo, 2 * s - 1)
-            xb_start(a, hi, 2 * s)
+            if a == 0:
+                xb_start(a, lo, 2 * s - 1)
+                xb_start(a, hi, 2 * s)
+            else:
+
+                @pl.when(s < LATE)
+                def _():
+                    xb_start(a, lo, 2 * s - 1)
+                    xb_start(a, hi, 2 * s)
+
 
         for a in range(2):
             sib_fwd(a, lo, 2 * s - 1).wait_recv()
@@ -161,7 +172,8 @@
         for u in range(2):
             ring_copy(a, a, 4, u).wait_recv()
         sib_fwd(a, far, 7).start()
-        xb_start(a, far, 7)
+        if a == 0:
+            xb_start(a, far, 7)
     for a in range(2):
         sib_fwd(a, far, 7).wait_recv()
         consume(a, far)
@@ -183,13 +195,29 @@
 
     lax.fori_loop(0, HID // 64, hidden_rows, 0)
 
-    def hq_copy(i, o):
-        blk = hq.at[i, x]
-        return remote(blk, blk, hq_s.at[i, o - 1], hq_r.at[i, o - 1], {"token": (x + o) % NX})
-
-    for i in range(3):
-        for o in range(1, NX):
-            hq_copy(i, o).start()
+    def piece(j):
+        return j // 2, pl.ds(j % 2 * HALF, HALF)
+
+    def hq_copy(j, d, hops):
+        i, units = piece(j)
+        src = x
+        if hops:
+            src = (x + NX - 1) % NX if d == 0 else (x + 1) % NX
+            units = pl.ds(j % 2 * HALF + d * (HALF // 2), HALF // 2)
+        blk = hq.at[i, src, units]
+        to = (x + 1) % NX if d == 0 else (x + NX - 1) % NX
+        return remote(blk, blk, hq_s.at[j, d, hops], hq_r.at[j, d, hops], {"token": to})
+
+    def hq_send(j):
+        for d in range(2):
+            hq_copy(j, d, 0).start()
+
+    def hq_relay(j):
+        for d in range(2):
+            hq_copy(j, d, 0).wait_recv()
+            hq_copy(j, d, 1).start()
+
+    hq_send(0)
 
     def rg_copy(a, o, half):
         blk = rg.at[a, c, (x + o) % NX, half]
@@ -199,34 +227,17 @@
         blk = rg.at[a, c, (x + o) % NX, half]
         return remote(blk, blk, xb_s.at[a, 0], xb_r.at[a, o - 1, half], sibling)
 
-    for a in range(2):
+    def rg_pass(a):
         for o in range(1, NX):
             for half in range(2):
                 rg_landed(a, o, half).wait_recv()
                 rg_copy(a, o, half).start()
 
-    dgb[...] = dgt[...].T
-    dub[...] = dut[...].T
-
-    def grad_block(zb, _):
-        at = pl.multiple_of(zb * ROWS, ROWS)
-        val = jnp.dot(dgb[...], wv[0, :, pl.ds(at, ROWS)], preferred_element_type=F32)
-        val += jnp.dot(dub[...], wv[1, :, pl.ds(at, ROWS)], preferred_element_type=F32)
-        val = val.astype(BF)
-        for yy in range(2):
-            for cc in range(2):
-                part[cc, zb, yy] = val[:, (yy * 2 + cc) * FEAT : (yy * 2 + cc + 1) * FEAT]
-        return 0
-
-    lax.fori_loop(0, NZ, grad_block, 0)
-    sib_part = remote(part.at[1 - c], sib, sb_s.at[0], sb_r.at[0], sibling)
-    sib_part.start()
-
     def square(v):
         v = v.astype(F32)
         return (v * v).astype(BF)
 
-    for a in range(2):
+    def squares(a):
         for o in range(NX):
             src = (x + o) % NX
             at = pl.multiple_of(src * TOK, TOK)
@@ -239,7 +250,51 @@
                         lane = (yy * 2 + cc) * FEAT
                         xs[a, half, pl.ds(at, TOK), lane : lane + FEAT] = square(v)
 
-    sib_part.wait_recv()
+    def f_copy(j):
+        i, units = piece(j)
+        return remote(fs.at[i, units], fr.at[i, units], f_s.at[j], f_r.at[j], mp_mate)
+
+    def hq_wait(j):
+        for d in range(2):
+            hq_copy(j, d, 1).wait_recv()
+
+    def fisher(j):
+        i, units = piece(j)
+        a = 1 if i == 2 else 0
+        lhs = jnp.concatenate([hq[i, t, units] for t in range(NX)], axis=1)
+        fs[i, units] = jnp.dot(lhs, xs[a, om_], preferred_element_type=F32).astype(BF)
+        f_copy(j).start()
+        fo = jnp.dot(lhs, xs[a, m], preferred_element_type=F32)
+        nown[i, units] = (fo * wv[i, units, merge_rows(m)].astype(F32)).astype(BF)
+        down[i, units] = fo.astype(BF)
+
+    dgb[...] = dgt[...].T
+    dub[...] = dut[...].T
+
+    def grad_block(zb, _):
+        at = pl.multiple_of(zb * ROWS, ROWS)
+        val = jnp.dot(dgb[...], wv[0, :, pl.ds(at, ROWS)], preferred_element_type=F32)
+        val += jnp.dot(dub[...], wv[1, :, pl.ds(at, ROWS)], preferred_element_type=F32)
+        val = val.astype(BF)
+        for yy in range(2):
+            for cc in range(2):
+                part[cc, zb, yy] = val[:, (yy * 2 + cc) * FEAT : (yy * 2 + cc + 1) * FEAT]
+        return 0
+
+    lax.fori_loop(0, NZ, grad_block, 0)
+    sib_part = remote(part.at[1 - c], sib, sb_s.at[0], sb_r.at[0], sibling)
+    sib_part.start()
+    hq_send(1)
+    hq_relay(0)
+    for s in range(LATE, 5):
+        for slot in (2 * s - 1, 2 * s) if s < 4 else (7,):
+            xb_start(1, wrap(z - s if slot % 2 else z + s), slot)
+    rg_pass(0)
+    squares(0)
+    hq_send(2)
+    hq_relay(1)
+    hq_wait(0)
+    fisher(0)
 
     def z_copy(o):
         to = (z + o) % NZ
@@ -249,26 +304,32 @@
         blk = zin.at[wrap(z - o)]
         return remote(blk, blk, z_s.at[o - 1], z_r.at[o - 1], tensor_at(wrap(z - o), yh, c))
 
+    sib_part.wait_recv()
     for o in range(1, NZ + 1):
         to = (z + o) % NZ
         sib[to] = (sib[to].astype(F32) + part[c, to].astype(F32)).astype(BF)
         if o < NZ:
             z_copy(o).start()
 
-    def f_copy(i):
-        return remote(fs.at[i], fr.at[i], f_s.at[i], f_r.at[i], mp_mate)
-
-    for i in range(3):
-        for o in range(1, NX):
-            blk = hq.at[i, (x - o + NX) % NX]
-            remote(blk, blk, hq_s.at[i, o - 1], hq_r.at[i, o - 1], {"token": (x - o + NX) % NX}).wait_recv()
-        a = 1 if i == 2 else 0
-        lhs = jnp.concatenate([hq[i, t] for t in range(NX)], axis=1)
-        fs[i] = jnp.dot(lhs, xs[a, om_], preferred_element_type=F32).astype(BF)
-        f_copy(i).start()
-        fo = jnp.dot(lhs, xs[a, m], preferred_element_type=F32)
-        nown[i] = (fo * wv[i, :, merge_rows(m)].astype(F32)).astype(BF)
-        down[i] = fo.astype(BF)
+    hq_send(3)
+    hq_relay(2)
+    hq_wait(1)
+    fisher(1)
+    hq_send(4)
+    hq_relay(3)
+    hq_wait(2)
+    fisher(2)
+    hq_send(5)
+    hq_relay(4)
+    rg_pass(1)
+    squares(1)
+    hq_wait(3)
+    fisher(3)
+    hq_relay(5)
+    hq_wait(4)
+    fisher(4)
+    hq_wait(5)
+    fisher(5)
 
     total = sib[z].astype(F32)
     for o in range(1, NZ):
@@ -278,21 +339,17 @@
     v_copy = remote(us.at[1 - yh], vin, v_s.at[0], v_r.at[0], y_mate)
     v_copy.start()
 
-    outs = []
     for i in range(3):
-        remote(fr.at[i], fr.at[i], f_s.at[i], f_r.at[i], mp_mate).wait_recv()
         remote(wr.at[i], wr.at[i], w_s.at[i], w_r.at[i], mp_mate).wait_recv()
-        if i == 2:
+    for j in range(PIECES):
+        i, units = piece(j)
+        f_copy(j).wait_recv()
+        if j == PIECES - 1:
             v_copy.wait_recv()
-            ogrd[...] = (us[yh].astype(F32) + vin[...].astype(F32)).astype(BF)
-            outs.append(pltpu.make_async_copy(ogrd, ig.at[0], out_sem.at[3]))
-            outs[-1].start()
-        other = fr[i].astype(F32)
-        num = nown[i].astype(F32) + (other * wr[i].astype(F32)).astype(BF).astype(F32)
-        merged = num / (down[i].astype(F32) + other)
-        om[i] = merged.astype(BF)
-        outs.append(pltpu.make_async_copy(om.at[i], mt.at[i], out_sem.at[i]))
-        outs[-1].start()
+            ig[0] = (us[yh].astype(F32) + vin[...].astype(F32)).astype(BF)
+        other = fr[i, units].astype(F32)
+        num = nown[i, units].astype(F32) + (other * wr[i, units].astype(F32)).astype(BF).astype(F32)
+        mt[i, units] = (num / (down[i, units].astype(F32) + other)).astype(BF)
 
     for a in range(2):
         yx_copy(a).wait_send()
@@ -314,15 +371,15 @@
                 rg_copy(a, o, half).wait_send()
     for i in range(3):
         w_copy(i).wait_send()
-        f_copy(i).wait_send()
-        for o in range(1, NX):
-            hq_copy(i, o).wait_send()
+    for j in range(PIECES):
+        f_copy(j).wait_send()
+        for d in range(2):
+            for hops in range(2):
+                hq_copy(j, d, hops).wait_send()
     sib_part.wait_send()
     for o in range(1, NZ):
         z_copy(o).wait_send()
     v_copy.wait_send()
-    for o in outs:
-        o.wait()
 
 
 def hand_out(ig, mt, ig_out, mg, mu, md, sem):
@@ -340,11 +397,11 @@
     ig, mt = pl.pallas_call(
         kernel,
         out_shape=(
-            jax.ShapeDtypeStruct((1, TOK, FEAT), BF),
-            jax.ShapeDtypeStruct((3, HID, ROWS), BF),
+            vm((1, TOK, FEAT), BF),
+            vm((3, HID, ROWS), BF),
         ),
         in_specs=[pl.BlockSpec(memory_space=pl.ANY)] * 5,
-        out_specs=[pl.BlockSpec(memory_space=pl.ANY)] * 2,
+        out_specs=[pl.BlockSpec(memory_space=pltpu.VMEM)] * 2,
         scratch_shapes=[
             vm((2, 2, NZ, 2, TOK, FEAT), BF),
             vm((2, 2, NX, 2, 2, TOK, FEAT), BF),
@@ -366,17 +423,15 @@
             vm((HID, TOK), BF),
             vm((TOK, HID), BF),
             vm((TOK, HID), BF),
-            vm((TOK, FEAT), BF),
-            vm((3, HID, ROWS), BF),
-            dma((5,)), dma((4,)),
+            dma((5,)),
             dma((2, 2, 5, 2)), dma((2, 2, 5, 2)),
             dma((2,)), dma((2,)),
             dma((2, 8)), dma((2, 8)),
             dma((2, 8)), dma((2, 3, 2)),
             dma((2, 3, 2)), dma((2, 3, 2)),
-            dma((3, 3)), dma((3, 3)),
+            dma((6, 2, 2)), dma((6, 2, 2)),
             dma((3,)), dma((3,)),
-            dma((3,)), dma((3,)),
+            dma((6,)), dma((6,)),
             dma((1,)), dma((1,)),
             dma((7,)), dma((7,)),
             dma((1,)), dma((1,)),
@@ -392,7 +447,7 @@
         out_specs=[pl.BlockSpec(memory_space=pl.ANY)] * 4,
         scratch_shapes=[dma((4,))],
         name="hand_out",
-    )(ig, mt)
+    )(*(pltpu.with_memory_space_constraint(v, pltpu.VMEM) for v in (ig, mt)))
     return ig, mg.T, mu.T, md
 
 

time: 101 us -> 93.2 us (0.923)
  the two profiles are of different devices: /device:TPU:42 before, /device:TPU:1 now
where the time goes in v3:
time: 93.2 us; the launch traced here: 93.1 us
  Pallas kernels  92.5 us (99%)
    pallas_call x1, Pallas kernels, local(): pl.pallas_call(kernel, out_shape=(vm((1, TOK, FEAT), BF), vm((3, HID, ROW...  91.4 us

profile of v3, /device:TPU:1, one launch (start us, length us, event | category | flops | bytes accessed | tf_op | source)
XLA Modules:
  0.0 93.1 jit_solution(13735596682157016042)
XLA Ops:
  0.6 91.4 %fisher_merge.1 = (bf16[1,256,128]{2,1,0:T(8,128)(2,1)S(1)}, bf16[3,448,512]{2,1,0:T(8,128)(2,1)S(1)}) custom-call(bf16[1,256,128]{2,1,0:T(8,128)(2,1)} %inp.1, bf16[1,256,128]{2,1,0:T(8,128)(2,1)} %cot.1, bf16[1,448,4096]{2,1,0:T(8,128)(2,1)} %bitcast.4, bf16[1,448,4096]{2,1,0:T(8,128)(2,1)} %bitcast.5, bf16[1,448,4096]{2,1,0:T(8,128)(2,1)} %dw.1), custom_call_target="tpu_custom_call" | custom-call | flops 7500000256 | bytes 16000000 | tf_op jit(solution)/shard_map/fisher_merge/pallas_call | solution.py:397
  92.0 1.1 %hand_out.1 = (bf16[1,256,128]{2,1,0:T(8,128)(2,1)}, bf16[448,512]{1,0:T(8,128)(2,1)}, bf16[448,512]{1,0:T(8,128)(2,1)}, bf16[448,512]{1,0:T(8,128)(2,1)}) custom-call(bf16[1,256,128]{2,1,0:T(8,128)(2,1)S(1)} %get-tuple-element.10.ig, bf16[3,448,512]{2,1,0:T(8,128)(2,1)S(1)} %get-tuple-element.11.mt), custom_call_target="tpu_custom_call" | custom-call | tf_op jit(solution)/shard_map/hand_out/pallas_call | solution.py:443

commit v4 on v3

--- a/solution.py
+++ b/solution.py
@@ -16,6 +16,7 @@
 NX = 4
 HALF = HID // 2
 PIECES = 6
+MERGED = 4
 LATE = 3
 NT = (((1,), (1,)), ((), ()))
 
@@ -217,7 +218,19 @@
             hq_copy(j, d, 0).wait_recv()
             hq_copy(j, d, 1).start()
 
+    def merge(j):
+        i, units = piece(j)
+        if j % 2 == 0:
+            remote(wr.at[i], wr.at[i], w_s.at[i], w_r.at[i], mp_mate).wait_recv()
+        f_copy(j).wait_recv()
+        other = fr[i, units].astype(F32)
+        num = nown[i, units].astype(F32) + (other * wr[i, units].astype(F32)).astype(BF).astype(F32)
+        mt[i, units] = (num / (down[i, units].astype(F32) + other)).astype(BF)
+
     hq_send(0)
+    for s in range(LATE, 5):
+        for slot in (2 * s - 1, 2 * s) if s < 4 else (7,):
+            xb_start(1, wrap(z - s if slot % 2 else z + s), slot)
 
     def rg_copy(a, o, half):
         blk = rg.at[a, c, (x + o) % NX, half]
@@ -286,16 +299,8 @@
     sib_part.start()
     hq_send(1)
     hq_relay(0)
-    for s in range(LATE, 5):
-        for slot in (2 * s - 1, 2 * s) if s < 4 else (7,):
-            xb_start(1, wrap(z - s if slot % 2 else z + s), slot)
     rg_pass(0)
     squares(0)
-    hq_send(2)
-    hq_relay(1)
-    hq_wait(0)
-    fisher(0)
-
     def z_copy(o):
         to = (z + o) % NZ
         return remote(sib.at[to], zin.at[z], z_s.at[o - 1], z_r.at[o - 1], tensor_at(to, yh, c))
@@ -304,12 +309,17 @@
         blk = zin.at[wrap(z - o)]
         return remote(blk, blk, z_s.at[o - 1], z_r.at[o - 1], tensor_at(wrap(z - o), yh, c))
 
+    hq_send(2)
+    hq_relay(1)
     sib_part.wait_recv()
     for o in range(1, NZ + 1):
         to = (z + o) % NZ
         sib[to] = (sib[to].astype(F32) + part[c, to].astype(F32)).astype(BF)
         if o < NZ:
             z_copy(o).start()
+
+    hq_wait(0)
+    fisher(0)
 
     hq_send(3)
     hq_relay(2)
@@ -321,15 +331,19 @@
     fisher(2)
     hq_send(5)
     hq_relay(4)
-    rg_pass(1)
-    squares(1)
     hq_wait(3)
     fisher(3)
     hq_relay(5)
+    merge(0)
+    rg_pass(1)
+    squares(1)
     hq_wait(4)
     fisher(4)
+    merge(1)
     hq_wait(5)
     fisher(5)
+    for j in range(2, MERGED):
+        merge(j)
 
     total = sib[z].astype(F32)
     for o in range(1, NZ):
@@ -339,17 +353,11 @@
     v_copy = remote(us.at[1 - yh], vin, v_s.at[0], v_r.at[0], y_mate)
     v_copy.start()
 
-    for i in range(3):
-        remote(wr.at[i], wr.at[i], w_s.at[i], w_r.at[i], mp_mate).wait_recv()
-    for j in range(PIECES):
-        i, units = piece(j)
-        f_copy(j).wait_recv()
+    for j in range(MERGED, PIECES):
         if j == PIECES - 1:
             v_copy.wait_recv()
             ig[0] = (us[yh].astype(F32) + vin[...].astype(F32)).astype(BF)
-        other = fr[i, units].astype(F32)
-        num = nown[i, units].astype(F32) + (other * wr[i, units].astype(F32)).astype(BF).astype(F32)
-        mt[i, units] = (num / (down[i, units].astype(F32) + other)).astype(BF)
+        merge(j)
 
     for a in range(2):
         yx_copy(a).wait_send()

time: 93.2 us -> 91 us (0.976)
  Pallas kernels: 92.5 us -> 90.3 us
    pallas_call x1, Pallas kernels: 91.4 us -> 89.2 us  [local(): pl.pallas_call(kernel, out_shape=(vm((1, TOK, FEAT), BF), vm((3, HID, ROW...]
where the time goes in v4:
time: 91 us; the launch traced here: 90.9 us
  Pallas kernels  90.3 us (99%)
    pallas_call x1, Pallas kernels, local(): pl.pallas_call(kernel, out_shape=(vm((1, TOK, FEAT), BF), vm((3, HID, ROW...  89.2 us

profile of v4, /device:TPU:1, one launch (start us, length us, event | category | flops | bytes accessed | tf_op | source)
XLA Modules:
  0.0 90.9 jit_solution(16187370857205517742)
XLA Ops:
  0.6 89.2 %fisher_merge.1 = (bf16[1,256,128]{2,1,0:T(8,128)(2,1)S(1)}, bf16[3,448,512]{2,1,0:T(8,128)(2,1)S(1)}) custom-call(bf16[1,256,128]{2,1,0:T(8,128)(2,1)} %inp.1, bf16[1,256,128]{2,1,0:T(8,128)(2,1)} %cot.1, bf16[1,448,4096]{2,1,0:T(8,128)(2,1)} %bitcast.4, bf16[1,448,4096]{2,1,0:T(8,128)(2,1)} %bitcast.5, bf16[1,448,4096]{2,1,0:T(8,128)(2,1)} %dw.1), custom_call_target="tpu_custom_call" | custom-call | flops 7500000256 | bytes 16000000 | tf_op jit(solution)/shard_map/fisher_merge/pallas_call | solution.py:405
  89.8 1.1 %hand_out.1 = (bf16[1,256,128]{2,1,0:T(8,128)(2,1)}, bf16[448,512]{1,0:T(8,128)(2,1)}, bf16[448,512]{1,0:T(8,128)(2,1)}, bf16[448,512]{1,0:T(8,128)(2,1)}) custom-call(bf16[1,256,128]{2,1,0:T(8,128)(2,1)S(1)} %get-tuple-element.10.ig, bf16[3,448,512]{2,1,0:T(8,128)(2,1)S(1)} %get-tuple-element.11.mt), custom_call_target="tpu_custom_call" | custom-call | tf_op jit(solution)/shard_map/hand_out/pallas_call | solution.py:451
